TPU v7x, 128 devices: a whole 4x4x4 slice. The times are simulated.
128 devices in a mesh: segment: 4 (over y_lo, core), hid: 16 (over x, z), wid: 2 (over y_hi).
Axes of the slice: x: 4, y: 4 (y_hi: 2, y_lo: 2; y = y_hi * 2 + y_lo), z: 4, core: 2. Of those that a mesh axis runs over, the one named last changes fastest.
Arguments:
- fwd_input: float32 [128, 5376], P('hid', 'wid'), may hold values from -90 to 90
- saved: float32 [4, 128, 5376], P('segment', 'hid', 'wid'), may hold values from -90 to 90
- cotan: float32 [128, 5376], P('hid', 'wid'), may hold values from -12 to 12
- norm_gain: float32 [4, 5376], P('segment', 'wid'), may hold values from 0.1 to 1.9
- w_gate: bfloat16 [4, 5376, 21504], P('segment', 'wid', 'hid'), may hold values from -0.078125 to 0.078125
- w_up: bfloat16 [4, 5376, 21504], P('segment', 'wid', 'hid'), may hold values from -1 to 1
- w_down: bfloat16 [4, 21504, 5376], P('segment', 'hid', 'wid'), may hold values from -1 to 1
- adapt_a: bfloat16 [4, 5376, 16], P('segment', 'wid'), may hold values from -0.078125 to 0.078125
- adapt_b: bfloat16 [4, 16, 21504], P('segment', None, 'hid'), may hold values from -1.5 to 1.5
Outputs:
- fwd_out: float32 [4, 128, 5376], P('segment', 'hid', 'wid')
- grad_in: float32 [4, 128, 5376], P('segment', 'hid', 'wid')
- grad_a: float32 [4, 5376, 16], P('segment', 'wid')
- grad_b: float32 [4, 16, 21504], P('segment', None, 'hid')
All inputs are finite; a program needn't handle non-finite values.
Results may differ from a plain program's by a relative error of at most 0.009.
Values may be sent and summed in bfloat16 or wider, within the bound.
A program may use at most 128 MiB of HBM per device.

v0:
```python
import jax
import jax.numpy as jnp
from jax import lax
from jax.sharding import PartitionSpec as P

D = 5376


epsilon = 1e-06
highest = lax.Precision.HIGHEST
ACROSS = (((1,), (1,)), ((), ()))
DOWN_ROWS = (((0,), (0,)), ((), ()))


def from_behind(block, axis, distance):
    devices = range(lax.axis_size(axis))
    route = [(i - distance, i) for i in devices if i - distance in devices]
    return lax.ppermute(block, axis, route)


def gelu_pair(values):
    active, pullback = jax.vjp(lambda inner: jax.nn.gelu(inner, approximate=True), values)
    return (active, pullback(jnp.ones_like(values))[0])


def guarded(enabled, making, blanks):
    return lax.cond(enabled, making, lambda: blanks)


def combine_units(pieces, adapter_b):
    gate_forward, up_forward, low_forward, gate_back, up_back, low_back, grad_hidden = pieces
    round_forward = low_forward.astype(jnp.bfloat16)
    up_total = up_forward + jnp.dot(round_forward, adapter_b, preferred_element_type=jnp.float32)
    hidden = (jax.nn.gelu(gate_forward, approximate=True) * up_total).astype(jnp.bfloat16)
    round_back = low_back.astype(jnp.bfloat16)
    up_full = up_back + jnp.dot(round_back, adapter_b, preferred_element_type=jnp.float32)
    active, slopes = gelu_pair(gate_back)
    grad_gate = (grad_hidden * up_full * slopes).astype(jnp.bfloat16)
    grad_up = (grad_hidden * active).astype(jnp.bfloat16)
    return (hidden, grad_gate, grad_up, round_back)


def body(fwd_input, saved, cotan, norm_gain, w_gate, w_up, w_down, adapt_a, adapt_b):
    segments = lax.axis_size("segment")
    section = lax.axis_index("segment")
    shards = lax.axis_size("hid")
    scales = norm_gain[0]
    gate_weights = w_gate[0]
    up_weights = w_up[0]
    down_weights = w_down[0]
    adapter_a = adapt_a[0]
    adapter_b = adapt_b[0]
    saved_rows = saved[0]
    part_rows, half_width = fwd_input.shape
    all_rows = part_rows * shards
    unit_count = gate_weights.shape[1]
    rank_count = adapter_a.shape[1]
    adapter_wide = adapter_a.astype(jnp.float32)
    saved_sum = lax.psum(jnp.sum(saved_rows * saved_rows, 1), "wid")
    saved_inverse = lax.rsqrt(saved_sum / D + epsilon)[:, None]
    saved_norm = lax.all_gather(
        (saved_rows * saved_inverse * scales).astype(jnp.bfloat16), "hid", axis=0, tiled=True
    )
    wide_blank = jnp.zeros((all_rows, unit_count), jnp.float32)
    thin_blank = jnp.zeros((all_rows, rank_count), jnp.float32)
    arrived_forward = jnp.zeros((part_rows, half_width), jnp.float32)
    arrived_backward = jnp.zeros((part_rows, half_width), jnp.float32)
    forward_kept = jnp.zeros((part_rows, half_width), jnp.float32)
    backward_kept = jnp.zeros((part_rows, half_width), jnp.float32)
    grad_a = jnp.zeros((half_width, rank_count), jnp.float32)
    grad_b = jnp.zeros((rank_count, unit_count), jnp.float32)
    for moment in range(segments):
        forward_on = section == moment
        backward_on = section == segments - 1 - moment
        current = jnp.where(section == 0, fwd_input, arrived_forward)
        grad_y = jnp.where(section == segments - 1, cotan, arrived_backward)
        current_sum = lax.psum(jnp.sum(current * current, 1), "wid")
        current_inverse = lax.rsqrt(current_sum / D + epsilon)[:, None]
        normed = (current * current_inverse * scales).astype(jnp.bfloat16)
        grad_round = grad_y.astype(jnp.bfloat16)
        active_rows = lax.all_gather(
            jnp.where(forward_on, normed, grad_round), "hid", axis=0, tiled=True
        )

        def forward_making():
            return (
                jnp.dot(active_rows, gate_weights, preferred_element_type=jnp.float32),
                jnp.dot(active_rows, up_weights, preferred_element_type=jnp.float32),
                jnp.dot(active_rows, adapter_a, preferred_element_type=jnp.float32),
                wide_blank,
            )

        def backward_making():
            return (
                jnp.dot(saved_norm, gate_weights, preferred_element_type=jnp.float32),
                jnp.dot(saved_norm, up_weights, preferred_element_type=jnp.float32),
                jnp.dot(saved_norm, adapter_a, preferred_element_type=jnp.float32),
                lax.dot_general(
                    active_rows, down_weights, ACROSS, preferred_element_type=jnp.float32
                ),
            )

        blanks = (wide_blank, wide_blank, thin_blank, wide_blank)
        terms = guarded(forward_on, forward_making, guarded(backward_on, backward_making, blanks))
        merged = lax.psum((terms[0], terms[1], terms[2], terms[3]), "wid")
        hidden, grad_gate, grad_up, round_back = combine_units(
            (merged[0], merged[1], merged[2], merged[0], merged[1], merged[2], merged[3]), adapter_b
        )
        grad_low = guarded(
            backward_on,
            lambda: lax.dot_general(grad_up, adapter_b, ACROSS, preferred_element_type=jnp.float32),
            thin_blank,
        )

        def down_block():
            return jnp.dot(hidden, down_weights, preferred_element_type=jnp.float32)

        def back_block():
            total = lax.dot_general(
                grad_gate, gate_weights, ACROSS, preferred_element_type=jnp.float32
            )
            total = total + lax.dot_general(
                grad_up, up_weights, ACROSS, preferred_element_type=jnp.float32
            )
            return total + jnp.dot(grad_low, adapter_wide.T, precision=highest)

        empty = jnp.zeros((part_rows * lax.axis_size("hid"), half_width), jnp.float32)
        either = lax.psum_scatter(
            guarded(
                forward_on, lambda: down_block(), guarded(backward_on, lambda: back_block(), empty)
            ),
            "hid",
            scatter_dimension=0,
            tiled=True,
        )
        produced = current + either
        weighted = lax.psum(jnp.sum(either * scales * saved_rows, 1), "wid")[:, None]
        cubed = saved_inverse * saved_inverse * saved_inverse
        grad_x = grad_y + saved_inverse * scales * either - saved_rows * cubed * weighted / D
        grad_a = grad_a + guarded(
            backward_on,
            lambda: jnp.dot(saved_norm.astype(jnp.float32).T, grad_low, precision=highest),
            jnp.zeros((half_width, rank_count), jnp.float32),
        )
        grad_b = grad_b + guarded(
            backward_on,
            lambda: lax.dot_general(
                round_back, grad_up, DOWN_ROWS, preferred_element_type=jnp.float32
            ),
            jnp.zeros((rank_count, unit_count), jnp.float32),
        )
        forward_kept = jnp.where(forward_on, produced, forward_kept)
        backward_kept = jnp.where(backward_on, grad_x, backward_kept)
        if moment + 1 < segments:
            arrived_forward = from_behind(produced, "segment", 1)
            arrived_backward = from_behind(grad_x, "segment", -1)
    grad_a = lax.psum(grad_a, "hid")
    return (forward_kept[None], backward_kept[None], grad_a[None], grad_b[None])


def solution(mesh):
    placed = (
        P("hid", "wid"),
        P("segment", "hid", "wid"),
        P("hid", "wid"),
        P("segment", "wid"),
        P("segment", "wid", "hid"),
        P("segment", "wid", "hid"),
        P("segment", "hid", "wid"),
        P("segment", "wid", None),
        P("segment", None, "hid"),
    )
    return jax.shard_map(
        body,
        mesh=mesh,
        in_specs=placed,
        out_specs=(
            P("segment", "hid", "wid"),
            P("segment", "hid", "wid"),
            P("segment", "wid", None),
            P("segment", None, "hid"),
        ),
        check_vma=False,
    )
```

profile of v0, /device:TPU:0, one launch (start us, length us, event | category | flops | bytes accessed | tf_op | source)
XLA Modules:
  0.0 972.7 jit_solution(3611869919868430362)
XLA Ops:
  7.2 1.1 fusion.42
  8.3 6.4 all-reduce.8
  15.5 1.0 fusion.49
  16.5 25.8 %all_gather.16 = bf16[128,2688]{1,0:T(8,128)(2,1)S(1)} all-gather(bf16[8,2688]{1,0:T(8,128)(2,1)S(1)} %fusion.49), channel_id=1, replica_groups=mesh['segment'=4,'hid'=16,'wid'=2] {'hid'}, dimensions={0}, use_global_device_ids=true | all-gather | bytes 731136 | tf_op jit(solution)/shard_map/all_gather | solution.py:81
  43.3 23.4 %all_gather.15 = bf16[128,2688]{1,0:T(8,128)(2,1)S(1)} all-gather(bf16[8,2688]{1,0:T(8,128)(2,1)S(1)} %fusion.44), channel_id=1, replica_groups=mesh['segment'=4,'hid'=16,'wid'=2] {'hid'}, dimensions={0}, use_global_device_ids=true | all-gather | bytes 731136 | tf_op jit(solution)/shard_map/all_gather | solution.py:61
  66.8 10.7 %copy.43 = bf16[1,2688,1344]{2,1,0:T(8,128)(2,1)} copy(bf16[1,2688,1344]{1,2,0:T(8,128)(2,1)} %param.69) | data formatting | bytes 14450688 | tf_op args[4]
  77.5 10.7 %copy.44 = bf16[1,2688,1344]{2,1,0:T(8,128)(2,1)} copy(bf16[1,2688,1344]{1,2,0:T(8,128)(2,1)} %param.70) | data formatting | bytes 14450688 | tf_op args[5]
  88.2 1.0 conditional.28
  89.2 11.1 %conditional.29 = ((f32[128,1344]{0,1:T(8,128)S(1)}, f32[128,1344]{0,1:T(8,128)S(1)}, f32[128,16]{0,1:T(8,128)S(1)}, f32[128,1344]{0,1:T(8,128)})) conditional(s32[]{:T(128)} %convert_element_type.63, (f32[128,1344]{0,1:T(8,128)S(1)}, f32[128,1344]{0,1:T(8,128)S(1)}, f32[128,16]{0,1:T(8,128)S(1)}, f32[128,1344]{0,1:T(8,128)}) %conditional.28, ...), branch_computations={%region_6.7_spmd, %region_7.8_spmd} | conditional | flops 1860698112 | bytes 47575112 | solution.py:27
  89.7 6.3 fusion.61
  96.0 3.1 fusion.62
  101.5 6.5 psum.186
  108.0 63.1 %all-reduce.36.cloned.1.call-done = (f32[128,1344]{0,1:T(8,128)}, f32[128,1344]{0,1:T(8,128)}, f32[128,1344]{0,1:T(8,128)}) async-done(((f32[128,1344]{0,1:T(8,128)}, f32[128,1344]{0,1:T(8,128)}, f32[128,1344]{0,1:T(8,128)}), (f32[128,1344]{0,1:T(8,128)}, f32[128,1344]{0,1:T(8,128)}, f32[128,1344]{0,1:T(8,128)})) %all-reduce.36.cloned.1.call-update) | async-done | bytes 2064400 | tf_op jit(solution)/shard_map/psum | solution.py:105
  171.1 3.0 multiply_convert_fusion.6
  174.3 4.6 conditional.32
  174.5 4.4 fusion.65
  178.9 1.1 copy-done.14
  181.3 92.4 %all-reduce.22.cloned.1.call-done = f32[128,2688]{1,0:T(8,128)} async-done(((f32[128,2688]{1,0:T(8,128)}), f32[128,2688]{1,0:T(8,128)}) %all-reduce.22.cloned.1.call-update) | async-done | bytes 1376272
  273.7 1.0 fusion.45
  274.7 1.3 collective-permute-start
  277.1 6.4 all-reduce.7
  284.5 1.3 collective-permute-start.1
  285.8 3.0 collective-permute-done.1
  288.9 23.9 %all_gather.17 = bf16[128,2688]{1,0:T(8,128)(2,1)S(1)} all-gather(bf16[8,2688]{1,0:T(8,128)(2,1)S(1)} %fusion.50), channel_id=1, replica_groups=mesh['segment'=4,'hid'=16,'wid'=2] {'hid'}, dimensions={0}, use_global_device_ids=true | all-gather | bytes 731136 | tf_op jit(solution)/shard_map/all_gather | solution.py:81
  312.8 1.0 conditional.33
  315.2 6.5 psum.192
  321.7 77.2 %all-reduce.34.cloned.1.call-done = (f32[128,1344]{0,1:T(8,128)}, f32[128,1344]{0,1:T(8,128)}, f32[128,1344]{0,1:T(8,128)}) async-done(((f32[128,1344]{0,1:T(8,128)}, f32[128,1344]{0,1:T(8,128)}, f32[128,1344]{0,1:T(8,128)}), (f32[128,1344]{0,1:T(8,128)}, f32[128,1344]{0,1:T(8,128)}, f32[128,1344]{0,1:T(8,128)})) %all-reduce.34.cloned.1.call-update) | async-done | bytes 2064400 | tf_op jit(solution)/shard_map/psum | solution.py:105
  398.9 3.0 multiply_convert_fusion.4
  402.5 1.1 copy-done.15
  403.7 98.5 %all-reduce.24.cloned.1.call-done = f32[128,2688]{1,0:T(8,128)} async-done(((f32[128,2688]{1,0:T(8,128)}), f32[128,2688]{1,0:T(8,128)}) %all-reduce.24.cloned.1.call-update) | async-done | bytes 1376272
  502.2 1.0 fusion.46
  503.3 1.3 collective-permute-start.2
  505.6 6.4 all-reduce.6
  513.0 1.3 collective-permute-start.3
  514.3 3.0 collective-permute-done.3
  517.5 23.9 %all_gather.18 = bf16[128,2688]{1,0:T(8,128)(2,1)S(1)} all-gather(bf16[8,2688]{1,0:T(8,128)(2,1)S(1)} %fusion.51), channel_id=1, replica_groups=mesh['segment'=4,'hid'=16,'wid'=2] {'hid'}, dimensions={0}, use_global_device_ids=true | all-gather | bytes 731136 | tf_op jit(solution)/shard_map/all_gather | solution.py:81
  541.3 1.0 conditional.38
  543.7 6.5 psum.198
  550.2 76.2 %all-reduce.32.cloned.1.call-done = (f32[128,1344]{0,1:T(8,128)}, f32[128,1344]{0,1:T(8,128)}, f32[128,1344]{0,1:T(8,128)}) async-done(((f32[128,1344]{0,1:T(8,128)}, f32[128,1344]{0,1:T(8,128)}, f32[128,1344]{0,1:T(8,128)}), (f32[128,1344]{0,1:T(8,128)}, f32[128,1344]{0,1:T(8,128)}, f32[128,1344]{0,1:T(8,128)})) %all-reduce.32.cloned.1.call-update) | async-done | bytes 2064400 | tf_op jit(solution)/shard_map/psum | solution.py:105
  626.4 3.0 multiply_convert_fusion.2
  629.7 1.1 copy-done.16
  630.9 97.5 %all-reduce.26.cloned.1.call-done = f32[128,2688]{1,0:T(8,128)} async-done(((f32[128,2688]{1,0:T(8,128)}), f32[128,2688]{1,0:T(8,128)}) %all-reduce.26.cloned.1.call-update) | async-done | bytes 1376272
  728.4 1.0 fusion.47
  729.4 1.3 collective-permute-start.4
  731.8 6.4 all-reduce.5
  739.2 1.3 collective-permute-start.5
  740.5 3.0 collective-permute-done.5
  743.6 23.9 %all_gather.19 = bf16[128,2688]{1,0:T(8,128)(2,1)S(1)} all-gather(bf16[8,2688]{1,0:T(8,128)(2,1)S(1)} %fusion.52), channel_id=1, replica_groups=mesh['segment'=4,'hid'=16,'wid'=2] {'hid'}, dimensions={0}, use_global_device_ids=true | all-gather | bytes 731136 | tf_op jit(solution)/shard_map/all_gather | solution.py:81
  767.5 12.7 %conditional.43 = (f32[128,1344]{0,1:T(8,128)S(1)}, f32[128,1344]{0,1:T(8,128)S(1)}, f32[128,16]{0,1:T(8,128)S(1)}, f32[128,1344]{0,1:T(8,128)}) conditional(s32[]{:T(128)} %convert_element_type.63, () %tuple.209, (bf16[128,2688]{1,0:T(8,128)(2,1)S(1)}, bf16[2688,1344]{1,0:T(8,128)(2,1)}, bf16[2688,1344]{1,0:T(8,128)(2,1)}, ...), branch_computations={%region_61.62_spmd, %region_62.63_spmd} | conditional | flops 2785542144 | bytes 77164656 | solution.py:27
  767.5 6.3 fusion.84
  773.8 3.1 fusion.85
  777.2 3.0 fusion.87
  781.8 6.5 psum.204
  788.3 62.1 %all-reduce.30.cloned.1.call-done = (f32[128,1344]{0,1:T(8,128)}, f32[128,1344]{0,1:T(8,128)}, f32[128,1344]{0,1:T(8,128)}) async-done(((f32[128,1344]{0,1:T(8,128)}, f32[128,1344]{0,1:T(8,128)}, f32[128,1344]{0,1:T(8,128)}), (f32[128,1344]{0,1:T(8,128)}, f32[128,1344]{0,1:T(8,128)}, f32[128,1344]{0,1:T(8,128)})) %all-reduce.30.cloned.1.call-update) | async-done | bytes 2064400 | tf_op jit(solution)/shard_map/psum | solution.py:105
  850.4 3.0 multiply_convert_fusion
  854.0 9.9 %conditional.46 = (f32[128,2688]{1,0:T(8,128)S(1)}) conditional(s32[]{:T(128)} %convert_element_type.63, () %tuple.208, (bf16[128,1344]{0,1:T(8,128)(2,1)}, bf16[2688,1344]{1,0:T(8,128)(2,1)}, bf16[128,1344]{0,1:T(8,128)(2,1)S(1)}, bf16[2688,1344]{1,0:T(8,128)(2,1)}, f32[128,16]{0,1:T(8,128)S(1)}, /*index=5*/f32[2688,16]{0,1:T(8,128)S(1)}) %tuple.415), branch_computations={%region_71.72_spmd, %region_72.73_spmd} | conditional | flops 1916436480 | bytes 51101732 | solution.py:27
  854.4 5.8 fusion.104
  860.2 2.5 convolution_add_fusion.7
  862.6 1.3 convolution_add_fusion.6
  867.1 86.9 %all-reduce.28.cloned.1.call-done = (f32[128,2688]{1,0:T(8,128)}, f32[1,2688,16]{1,2,0:T(8,128)}) async-done(((f32[128,2688]{1,0:T(8,128)}, f32[1,2688,16]{1,2,0:T(8,128)}), (f32[128,2688]{1,0:T(8,128)}, f32[1,2688,16]{1,2,0:T(8,128)})) %all-reduce.28.cloned.1.call-update) | async-done | bytes 1548304
  954.0 1.7 fusion.48
  955.7 6.4 psum.206
  962.1 1.7 fusion.41
  963.8 1.6 copy.222
  (174 shorter events, 24.3 us)
Async XLA Ops:
  7.2 163.9 %all-reduce.36.cloned.1.call-start = ((), (), s32[]{:S(2)}) async-start(), calls=%async_computation.7 | async-start | bytes 4128768 | tf_op jit(solution)/shard_map/psum | solution.py:105
  42.3 695.9 %copy-start.47 = (f32[8]{0:T(128)}, f32[8]{0:T(128)S(1)}, u32[]{:S(2)}) copy-start(f32[8]{0:T(128)S(1)} %get-tuple-element.600) | copy-start | bytes 100
  77.5 10.7 %copy-start.13 = (bf16[1,2688,16]{1,2,0:T(8,128)(2,1)S(1)}, bf16[1,2688,16]{1,2,0:T(8,128)(2,1)}, u32[]{:S(2)}) copy-start(bf16[1,2688,16]{1,2,0:T(8,128)(2,1)} %param.72) | copy-start | bytes 258052
  89.2 81.9 %copy-start.28 = (bf16[1,16,1344]{2,1,0:T(8,128)(2,1)S(1)}, bf16[1,16,1344]{2,1,0:T(8,128)(2,1)}, u32[]{:S(2)}) copy-start(bf16[1,16,1344]{2,1,0:T(8,128)(2,1)} %param.73) | copy-start | bytes 129028
  89.7 6.3 copy-start.1
  100.3 0.8 copy-start.20
  100.3 1.1 copy-start.21
  101.4 172.2 %all-reduce.22.cloned.1.call-start = ((), (), s32[]{:S(2)}) async-start(), calls=%async_computation | async-start | bytes 2752512
  174.2 5.8 copy-start.49
  174.2 99.5 %copy-start.12 = (f32[1,8,2688]{2,1,0:T(8,128)S(1)}, f32[1,8,2688]{2,1,0:T(8,128)}, u32[]{:S(2)}) copy-start(f32[1,8,2688]{2,1,0:T(8,128)} %param.66) | copy-start | bytes 258052
  174.2 99.4 %copy-start.19 = (f32[8,2688]{1,0:T(8,128)S(1)}, f32[8,2688]{1,0:T(8,128)}, u32[]{:S(2)}) copy-start(f32[8,2688]{1,0:T(8,128)} %param.65) | copy-start | bytes 258052
  174.3 109.3 %copy-start.18 = (f32[8,2688]{1,0:T(8,128)S(1)}, f32[8,2688]{1,0:T(8,128)}, u32[]{:S(2)}) copy-start(f32[8,2688]{1,0:T(8,128)} %param.67) | copy-start | bytes 258052
  178.8 1.1 copy-start.14
  180.0 219.0 %all-reduce.34.cloned.1.call-start = ((), (), s32[]{:S(2)}) async-start(), calls=%async_computation.6 | async-start | bytes 4128768 | tf_op jit(solution)/shard_map/psum | solution.py:105
  274.7 1.3 copy-start.35
  274.7 2.2 collective-permute-start
  284.5 28.3 %copy-start.41 = (f32[8,2688]{1,0:T(8,128)}, f32[8,2688]{1,0:T(8,128)S(1)}, u32[]{:S(2)}) copy-start(f32[8,2688]{1,0:T(8,128)S(1)} %fusion.33) | copy-start | bytes 258052
  284.5 4.3 collective-permute-start.1
  314.0 0.8 copy-start.22
  314.0 1.1 copy-start.23
  315.1 187.1 %all-reduce.24.cloned.1.call-start = ((), (), s32[]{:S(2)}) async-start(), calls=%async_computation.1 | async-start | bytes 2752512
  402.5 1.1 copy-start.15
  403.6 222.7 %all-reduce.32.cloned.1.call-start = ((), (), s32[]{:S(2)}) async-start(), calls=%async_computation.5 | async-start | bytes 4128768 | tf_op jit(solution)/shard_map/psum | solution.py:105
  503.3 38.1 %copy-start.37 = (f32[8,2688]{1,0:T(8,128)}, f32[8,2688]{1,0:T(8,128)S(1)}, u32[]{:S(2)}) copy-start(f32[8,2688]{1,0:T(8,128)S(1)} %get-tuple-element.591) | copy-start | bytes 258052
  503.3 2.2 collective-permute-start.2
  513.0 28.3 %copy-start.43 = (f32[8,2688]{1,0:T(8,128)}, f32[8,2688]{1,0:T(8,128)S(1)}, u32[]{:S(2)}) copy-start(f32[8,2688]{1,0:T(8,128)S(1)} %fusion.35) | copy-start | bytes 258052
  513.0 4.3 collective-permute-start.3
  542.5 0.8 copy-start.24
  542.5 1.1 copy-start.25
  543.6 184.7 %all-reduce.26.cloned.1.call-start = ((), (), s32[]{:S(2)}) async-start(), calls=%async_computation.2 | async-start | bytes 2752512
  629.7 1.1 copy-start.16
  630.9 219.5 %all-reduce.30.cloned.1.call-start = ((), (), s32[]{:S(2)}) async-start(), calls=%async_computation.4 | async-start | bytes 4128768 | tf_op jit(solution)/shard_map/psum | solution.py:105
  729.4 38.1 %copy-start.39 = (f32[8,2688]{1,0:T(8,128)}, f32[8,2688]{1,0:T(8,128)S(1)}, u32[]{:S(2)}) copy-start(f32[8,2688]{1,0:T(8,128)S(1)} %get-tuple-element.586) | copy-start | bytes 258052
  729.4 2.2 collective-permute-start.4
  739.2 28.3 %copy-start.45 = (f32[8,2688]{1,0:T(8,128)}, f32[8,2688]{1,0:T(8,128)S(1)}, u32[]{:S(2)}) copy-start(f32[8,2688]{1,0:T(8,128)S(1)} %fusion.37) | copy-start | bytes 258052
  739.2 4.3 collective-permute-start.5
  743.5 23.9 %copy-start.46 = (f32[8,2688]{1,0:T(8,128)}, f32[8,2688]{1,0:T(8,128)S(1)}, u32[]{:S(2)}) copy-start(f32[8,2688]{1,0:T(8,128)S(1)} %collective-permute-done.5) | copy-start | bytes 258052
  767.5 6.3 copy-start.9
  767.5 9.6 slice-start.6
  773.8 3.4 slice-start.7
  780.4 0.8 copy-start.26
  780.5 1.1 copy-start.27
  781.6 172.4 %all-reduce.28.cloned.1.call-start = ((), (), s32[]{:S(2)}) async-start(), calls=%async_computation.3 | async-start | bytes 3096576
  781.6 72.4 %copy-start.29 = (f32[2688,16]{0,1:T(8,128)}, f32[2688,16]{0,1:T(8,128)S(1)}, u32[]{:S(2)}) copy-start(f32[2688,16]{0,1:T(8,128)S(1)} %get-tuple-element.702) | copy-start | bytes 516100
  781.7 72.3 %copy-start.31 = (f32[2688,16]{0,1:T(8,128)}, f32[2688,16]{0,1:T(8,128)S(1)}, u32[]{:S(2)}) copy-start(f32[2688,16]{0,1:T(8,128)S(1)} %get-tuple-element.703) | copy-start | bytes 516100
  781.8 72.3 %copy-start.33 = (f32[2688,16]{0,1:T(8,128)}, f32[2688,16]{0,1:T(8,128)S(1)}, u32[]{:S(2)}) copy-start(f32[2688,16]{0,1:T(8,128)S(1)} %get-tuple-element.704) | copy-start | bytes 516100
  854.3 5.8 copy-start.11
  863.9 0.9 copy-start.30
  864.0 1.1 copy-start.32
  864.0 1.4 copy-start.34
  864.0 90.0 %copy-start.36 = (f32[8,2688]{1,0:T(8,128)S(1)}, f32[8,2688]{1,0:T(8,128)}, u32[]{:S(2)}) copy-start(f32[8,2688]{1,0:T(8,128)} %copy-done.35) | copy-start | bytes 258052
  864.0 90.0 %copy-start.38 = (f32[8,2688]{1,0:T(8,128)S(1)}, f32[8,2688]{1,0:T(8,128)}, u32[]{:S(2)}) copy-start(f32[8,2688]{1,0:T(8,128)} %copy-done.37) | copy-start | bytes 258052
  864.0 90.0 %copy-start.40 = (f32[8,2688]{1,0:T(8,128)S(1)}, f32[8,2688]{1,0:T(8,128)}, u32[]{:S(2)}) copy-start(f32[8,2688]{1,0:T(8,128)} %copy-done.39) | copy-start | bytes 258052
  864.0 98.1 %copy-start.42 = (f32[8,2688]{1,0:T(8,128)S(1)}, f32[8,2688]{1,0:T(8,128)}, u32[]{:S(2)}) copy-start(f32[8,2688]{1,0:T(8,128)} %copy-done.41) | copy-start | bytes 258052
  864.0 98.1 %copy-start.44 = (f32[8,2688]{1,0:T(8,128)S(1)}, f32[8,2688]{1,0:T(8,128)}, u32[]{:S(2)}) copy-start(f32[8,2688]{1,0:T(8,128)} %copy-done.43) | copy-start | bytes 258052
  864.0 98.1 %copy-start.48 = (f32[8]{0:T(128)S(1)}, f32[8]{0:T(128)}, u32[]{:S(2)}) copy-start(f32[8]{0:T(128)} %copy-done.47) | copy-start | bytes 100
  864.1 2.0 copy-start.17
Sparse Core Ops, SparseCore 0:
  101.6 69.4 all-reduce.35
  180.1 93.5 all-reduce.21
  315.2 83.6 all-reduce.33
  403.8 98.4 all-reduce.23
  543.8 82.5 all-reduce.31
  631.0 97.3 all-reduce.25
  781.7 68.6 all-reduce.29
  866.2 87.7 all-reduce.27
where the time goes:
time: 981 us; the launch traced here: 973 us
  waiting for transfers between devices  666 us (68%)
  blocking collectives  179 us (18%)
  matrix products  49 us (5%)
  local copies, waits for them, and re-layouts  37 us (4%)
  between operations  15.9 us (2%)
  other arithmetic  15.3 us (2%)
    unnamed x12, waiting for transfers between devices  375 us
    psum x4, waiting for transfers between devices, body(): merged = lax.psum((terms[0], terms[1], terms[2], terms[3]), 'wid')  279 us
    all_gather x4, blocking collectives, body(): lax.all_gather(jnp.where(forward_on, normed, grad_round), 'hid', axis=0,...  97.4 us
    unnamed x80, local copies, waits for them, and re-layouts  32.6 us
    psum x4, blocking collectives, body(): merged = lax.psum((terms[0], terms[1], terms[2], terms[3]), 'wid')  26.1 us
    all_gather x1, blocking collectives, body(): lax.all_gather((saved_rows * saved_inverse * scales).astype(jnp.bfloat16)...  23.4 us
  transfers between devices with their start and end apart: 14, of which 14 were waited for; matrix products, arithmetic and copies ran while one was open for 0% of the time, Pallas kernels for 0%

commit v1 on v0

v1 whole, which is shorter than its diff:
```python
import functools
import math

import jax
import jax.numpy as jnp
from jax import lax
from jax.experimental import pallas as pl
from jax.experimental.pallas import tpu as pltpu
from jax.sharding import PartitionSpec as P

EPSILON = 1e-06
LANES = 128
UNIT_STEP = 512
WIDTH_STEP = 1024
ROOT = math.sqrt(2.0 / math.pi)
CUBE = 0.044715
MESH = pl.DeviceIdType.MESH
ACROSS = (((1,), (1,)), ((), ()))
F32 = jnp.float32
B16 = jnp.bfloat16


def cuts(total, step):
    return [(at, min(step, total - at)) for at in range(0, total, step)]


def up_to(size, step):
    return (size + step - 1) // step * step


def dot(a, b):
    return jnp.dot(a, b, preferred_element_type=F32)


def dot_across(a, b):
    return lax.dot_general(a, b, ACROSS, preferred_element_type=F32)


def two_parts(value):
    high = value.astype(B16).astype(F32)
    return high, value - high


def tail_of(value):
    high, low = two_parts(value)
    lane = lax.broadcasted_iota(jnp.int32, (value.shape[0], LANES), 1)
    return jnp.where(lane == 16, high, jnp.where(lane == 17, low, 0.0))


def kernel(sizes, *refs):
    segments, shards, width, units, rank = sizes
    (fwd_input, saved, cotan, gain, gate_hbm, up_hbm, down_hbm, adapt_a, adapt_b) = refs[:9]
    (fwd_out, grad_in, grad_a, grad_b) = refs[9:13]
    (
        w_gate, w_up, w_down, a_pad, b_pad,
        rows_f, rows_s, rows_b, flat,
        part_f, got_f, part_s, got_s, part_b, got_b,
        low_f, low_got_f, low_s, low_got_s, low_round, low_turned, inverse,
        extra, hidden, d_gate, d_up, slope_term, active_term, inner_term, inner,
        sum_f, back_f, sum_b, back_b,
        thin, thin_got, x_in, g_in, gain_here, gain_next,
        first_message, saved_message, next_message, y_out, g_out,
        sends, recvs, loads,
    ) = refs[13:]
    section = lax.axis_index("segment")
    me = lax.axis_index("hid")
    side = lax.axis_index("wid")
    part = 8
    rows = part * shards
    full = width * 2
    unit_cuts = cuts(units, UNIT_STEP)
    width_cuts = cuts(width, WIDTH_STEP)
    nu, nw = len(unit_cuts), len(width_cuts)
    at = 0
    GF, GS, GB, THIN, XIN, GIN, GAIN = range(7)
    XF = 7
    XS = XF + 1 + 2 * nu
    XB = XS + 1 + 2 * nu
    RF = XB + nu
    RB = RF + nw

    def take(ref, sem):
        pltpu.make_async_copy(ref, ref, sem).wait()

    def weights(index):
        source, target = ((gate_hbm, w_gate), (up_hbm, w_up), (down_hbm, w_down))[index]
        return pltpu.make_async_copy(source.at[0], target, loads.at[index])

    for index in range(3):
        weights(index).start()

    barrier = pltpu.get_barrier_semaphore()

    def greet(who):
        pl.semaphore_signal(barrier, inc=1, device_id=who, device_id_type=MESH)

    def greet_peer(i, carry):
        greet({"hid": lax.rem(me + i, shards)})
        return carry

    lax.fori_loop(1, shards, greet_peer, 0)
    greet({"wid": 1 - side})

    @pl.when(section > 0)
    def _():
        def one(i, carry):
            greet({"segment": section - 1, "hid": lax.rem(me + i, shards)})
            return carry

        lax.fori_loop(0, shards, one, 0)

    @pl.when(section < segments - 1)
    def _():
        def one(i, carry):
            greet({"segment": section + 1, "hid": lax.rem(me + i, shards)})
            return carry

        lax.fori_loop(0, shards, one, 0)

    scales = gain[...]
    gain_here[...] = jnp.broadcast_to(scales, (part, width))

    def message(ref, values, column):
        ref[:, :width] = values.astype(B16)
        ref[:, width:] = tail_of(column).astype(B16)

    saved_rows = saved[0]

    @pl.when(section == 0)
    def _():
        x = fwd_input[...]
        x_in[...] = x
        message(first_message, x * scales, jnp.sum(x * x, axis=1, keepdims=True))

    @pl.when(section == segments - 1)
    def _():
        g = cotan[...]
        g_in[...] = g
        message(first_message, g, jnp.zeros((part, 1), F32))

    message(saved_message, saved_rows * scales, jnp.sum(saved_rows * saved_rows, axis=1, keepdims=True))

    neighbours = jnp.where(section > 0, shards, 0) + jnp.where(section < segments - 1, shards, 0)
    pl.semaphore_wait(barrier, shards + neighbours)

    def spread(source, target, index):
        pltpu.make_async_copy(source, target.at[me], recvs.at[index]).start()

        def one(i, carry):
            pltpu.make_async_remote_copy(
                src_ref=source, dst_ref=target.at[me],
                send_sem=sends.at[index], recv_sem=recvs.at[index],
                device_id={"hid": lax.rem(me + i, shards)}, device_id_type=MESH,
            ).start()
            return carry

        lax.fori_loop(1, shards, one, 0)

    def spread_to(other, source, target, index):
        def one(i, carry):
            pltpu.make_async_remote_copy(
                src_ref=source, dst_ref=target.at[me],
                send_sem=sends.at[index], recv_sem=recvs.at[index],
                device_id={"segment": other, "hid": lax.rem(me + i, shards)}, device_id_type=MESH,
            ).start()
            return carry

        lax.fori_loop(0, shards, one, 0)

    def deliver(source, target, index, columns):
        pltpu.make_async_copy(
            source.at[me, :, columns], target.at[me, :, columns], recvs.at[index]
        ).start()

        def one(i, carry):
            peer = lax.rem(me + i, shards)
            pltpu.make_async_remote_copy(
                src_ref=source.at[peer, :, columns], dst_ref=target.at[me, :, columns],
                send_sem=sends.at[index], recv_sem=recvs.at[index],
                device_id={"hid": peer}, device_id_type=MESH,
            ).start()
            return carry

        lax.fori_loop(1, shards, one, 0)

    def across(source, target, index):
        return pltpu.make_async_remote_copy(
            src_ref=source, dst_ref=target,
            send_sem=sends.at[index], recv_sem=recvs.at[index],
            device_id={"wid": 1 - side}, device_id_type=MESH,
        )

    def onward(other, source, target, index):
        return pltpu.make_async_remote_copy(
            src_ref=source, dst_ref=target,
            send_sem=sends.at[index], recv_sem=recvs.at[index],
            device_id={"segment": other}, device_id_type=MESH,
        )

    @pl.when(section == 0)
    def _():
        spread(first_message, rows_f, GF)

    @pl.when(section == segments - 1)
    def _():
        spread(first_message, rows_b, GB)

    spread(saved_message, rows_s, GS)

    @pl.when(section > 0)
    def _():
        onward(section - 1, gain_here, gain_next, GAIN).start()

    a_pad[...] = jnp.zeros_like(a_pad)
    a_pad[:, :rank] = adapt_a[0]
    b_pad[...] = jnp.zeros_like(b_pad)
    b_pad[:rank, :] = adapt_b[0]
    wide = part_f.shape[2]
    last = units // LANES * LANES
    if last < wide:
        for buffer in (part_f, part_s):
            for j in range(2):
                buffer[j, :, last:] = jnp.zeros((rows, wide - last), B16)
        part_b[:, last:] = jnp.zeros((rows, wide - last), B16)

    def flatten(source):
        def one(i, carry):
            pair = [source[2 * i + j, :, :width].astype(F32) for j in range(2)]
            flat[pl.ds(pl.multiple_of(i * 16, 16), 16), :] = jnp.concatenate(pair, 0).astype(B16)
            return carry

        lax.fori_loop(0, shards // 2, one, 0)

    def cut_of(buffer, start, size):
        return buffer[:, pl.ds(start, up_to(size, LANES))]

    def span(start, size):
        return pl.ds(start, up_to(size, LANES))

    def project(gathered, sem, mine, theirs, low_mine, low_theirs, base):
        take(gathered, recvs.at[sem])
        flatten(gathered)
        tail = gathered[:, :, width:].astype(F32).reshape(rows, LANES)
        low_mine[...] = (dot(flat[...], a_pad[...]) + tail).astype(B16)
        across(low_mine, low_theirs, base).start()
        for c, (start, size) in enumerate(unit_cuts):
            for j, matrix in enumerate((w_gate, w_up)):
                mine[j, :, start : start + size] = dot(
                    flat[...], matrix[:, start : start + size]
                ).astype(B16)
                across(
                    mine.at[j, :, span(start, size)],
                    theirs.at[j, :, span(start, size)],
                    base + 1 + 2 * c + j,
                ).start()

    def join_low(low_mine, low_theirs, base):
        take(low_theirs, recvs.at[base])
        low = low_mine[...].astype(F32) + low_theirs[...].astype(F32)
        squares = low[:, 16:17] + low[:, 17:18]
        inv = lax.rsqrt(squares / full + EPSILON)
        inverse[...] = jnp.broadcast_to(inv, (rows, LANES))
        lane = lax.broadcasted_iota(jnp.int32, (rows, LANES), 1)
        low = jnp.where(lane < rank, low * inv, 0.0)
        low_round[...] = low.astype(B16)
        return low

    def each_block(work):
        def one(i, carry):
            work(pl.ds(pl.multiple_of(i * 16, 16), 16))
            return carry

        lax.fori_loop(0, rows // 16, one, 0)

    def join_units(mine, theirs, base, work):
        for c, (start, size) in enumerate(unit_cuts):
            for j in range(2):
                take(theirs.at[j, :, span(start, size)], recvs.at[base + 1 + 2 * c + j])
            extra[:, :size] = dot(low_round[...], b_pad[:, start : start + size])
            here = slice(start, start + size)

            def block(at_rows):
                inv = inverse[at_rows, :1]
                gate = mine[0, at_rows, here].astype(F32) + theirs[0, at_rows, here].astype(F32)
                up = mine[1, at_rows, here].astype(F32) + theirs[1, at_rows, here].astype(F32)
                work(at_rows, here, gate * inv, up * inv + extra[at_rows, :size])

            each_block(block)

    def total(received, index, take_columns):
        for c, (start, size) in enumerate(width_cuts):
            more = take_columns(c)
            take(received.at[:, :, pl.ds(start, size + more)], recvs.at[index + c])
            value = received[0, :, start : start + size + more].astype(F32)
            for k in range(1, shards):
                value = value + received[k, :, start : start + size + more].astype(F32)
            yield start, size, value

    def forward():
        project(rows_f, GF, part_f, got_f, low_f, low_got_f, XF)
        join_low(low_f, low_got_f, XF)

        def work(at_rows, here, gate, up):
            bend = jnp.tanh(ROOT * (gate + CUBE * gate * gate * gate))
            hidden[at_rows, here] = (0.5 * gate * (1.0 + bend) * up).astype(B16)

        join_units(part_f, got_f, XF, work)
        for c, (start, size) in enumerate(width_cuts):
            value = dot(hidden[...], w_down[:, start : start + size])
            sum_f[:, :, start : start + size] = value.reshape(shards, part, size).astype(B16)
            deliver(sum_f, back_f, RF + c, pl.ds(start, size))

        @pl.when(section > 0)
        def _():
            take(x_in, recvs.at[XIN])

        squares = jnp.zeros((part, 1), F32)

        @pl.when(section < segments - 1)
        def _():
            take(gain_next, recvs.at[GAIN])

        for start, size, value in total(back_f, RF, lambda c: 0):
            y = x_in[:, start : start + size] + value
            y_out[:, start : start + size] = y
            squares = squares + jnp.sum(y * y, axis=1, keepdims=True)

        @pl.when(section < segments - 1)
        def _():
            message(next_message.at[0], y_out[...] * gain_next[...], squares)
            spread_to(section + 1, next_message.at[0], rows_f, GF)
            onward(section + 1, y_out, x_in, XIN).start()

        fwd_out[0] = y_out[...]

    def recompute():
        project(rows_s, GS, part_s, got_s, low_s, low_got_s, XS)
        low = join_low(low_s, low_got_s, XS)
        low_turned[...] = low.T.astype(B16)

        def work(at_rows, here, gate, up):
            bend = jnp.tanh(ROOT * (gate + CUBE * gate * gate * gate))
            active = 0.5 * gate * (1.0 + bend)
            slope = 0.5 * (1.0 + bend) + 0.5 * gate * (1.0 - bend * bend) * (
                ROOT * (1.0 + 3.0 * CUBE * gate * gate)
            )
            steep = up * slope
            slope_term[at_rows, here] = steep
            active_term[at_rows, here] = active
            inner_term[at_rows, here] = steep * gate + active * up

        join_units(part_s, got_s, XS, work)
        inverse_saved = inner.at[1]
        inverse_saved[...] = inverse[...]

    def backward():
        take(rows_b, recvs.at[GB])
        flatten(rows_b)
        for c, (start, size) in enumerate(unit_cuts):
            part_b[:, start : start + size] = dot_across(
                flat[...], w_down[start : start + size, :]
            ).astype(B16)
            across(
                part_b.at[:, span(start, size)], got_b.at[:, span(start, size)], XB + c
            ).start()
        inner[0] = jnp.zeros((rows, LANES), F32)
        for c, (start, size) in enumerate(unit_cuts):
            take(got_b.at[:, span(start, size)], recvs.at[XB + c])
            here = slice(start, start + size)

            def block(at_rows):
                d_hid = part_b[at_rows, here].astype(F32) + got_b[at_rows, here].astype(F32)
                d_gate[at_rows, here] = (d_hid * slope_term[at_rows, here]).astype(B16)
                d_up[at_rows, here] = (d_hid * active_term[at_rows, here]).astype(B16)
                inner[0, at_rows, :] += jnp.broadcast_to(
                    jnp.sum(d_hid * inner_term[at_rows, here], axis=1, keepdims=True), (16, LANES)
                )

            each_block(block)
        d_low = dot_across(d_up[...], b_pad[...])
        d_low_round = d_low.astype(B16)
        thin_mine = (d_low * inner[1]).T[:rank]
        thin[...] = thin_mine

        def one(i, carry):
            pltpu.make_async_remote_copy(
                src_ref=thin, dst_ref=thin_got.at[me],
                send_sem=sends.at[THIN], recv_sem=recvs.at[THIN],
                device_id={"hid": lax.rem(me + i, shards)}, device_id_type=MESH,
            ).start()
            return carry

        tail = tail_of(inner[0][:, :1])
        sum_b[:, :, width:] = tail.reshape(shards, part, LANES).astype(B16)
        for c, (start, size) in enumerate(width_cuts):
            value = dot_across(d_gate[...], w_gate[start : start + size, :])
            value = value + dot_across(d_up[...], w_up[start : start + size, :])
            value = value + dot_across(d_low_round, a_pad[start : start + size, :])
            sum_b[:, :, start : start + size] = value.reshape(shards, part, size).astype(B16)
            more = LANES if c == nw - 1 else 0
            deliver(sum_b, back_b, RB + c, pl.ds(start, size + more))
        pltpu.make_async_copy(thin, thin_got.at[me], recvs.at[THIN]).start()
        lax.fori_loop(1, shards, one, 0)
        grad_b[0] = dot(low_turned[...], d_up[...])[:rank]

        @pl.when(section < segments - 1)
        def _():
            take(g_in, recvs.at[GIN])

        inv = inner[1, pl.ds(pl.multiple_of(me * part, part), part), :][:, :1]
        parts = list(total(back_b, RB, lambda c: LANES if c == nw - 1 else 0))
        start, size, value = parts[-1]
        weight = value[:, size + 16 : size + 17] + value[:, size + 17 : size + 18]
        weight = inv * inv * weight / full
        for start, size, value in parts:
            here = slice(start, start + size)
            g_out[:, here] = (
                g_in[:, here]
                + inv * gain_here[:, here] * value[:, :size]
                - saved[0, :, here] * weight
            )

        @pl.when(section > 0)
        def _():
            message(next_message.at[1], g_out[...], jnp.zeros((part, 1), F32))
            spread_to(section - 1, next_message.at[1], rows_b, GB)
            onward(section - 1, g_out, g_in, GIN).start()

        grad_in[0] = g_out[...]
        take(thin_got, recvs.at[THIN])
        low_sum = thin_got[0]
        for k in range(1, shards):
            low_sum = low_sum + thin_got[k]
        high, low = two_parts(low_sum)
        flatten(rows_s)
        turned = dot(high.astype(B16), flat[...]) + dot(low.astype(B16), flat[...])
        for at_lane in range(0, width, LANES):
            block = jnp.concatenate(
                [turned[:, at_lane : at_lane + LANES], jnp.zeros((LANES - rank, LANES), F32)], 0
            )
            grad_a[0, at_lane : at_lane + LANES, :] = block.T[:, :rank]

    for index in range(3):
        weights(index).wait()

    def moment(now, carry):
        pl.when(section == now)(forward)
        pl.when(now == 0)(recompute)
        pl.when(section == segments - 1 - now)(backward)
        return carry

    lax.fori_loop(0, segments, moment, 0)

    def sent(ref, index):
        take(ref, sends.at[index])

    others = pl.ds(0, shards - 1)

    @pl.when(section == 0)
    def _():
        sent(rows_f.at[others], GF)
        sent(rows_f, GF)

    @pl.when(jnp.logical_and(section > 0, section < segments - 1))
    def _():
        sent(rows_f, GF)
        sent(rows_b, GB)

    @pl.when(section == segments - 1)
    def _():
        sent(rows_b.at[others], GB)
        sent(rows_b, GB)

    @pl.when(section > 0)
    def _():
        sent(gain_here, GAIN)
        sent(g_out, GIN)

    @pl.when(section < segments - 1)
    def _():
        sent(y_out, XIN)

    sent(rows_s.at[others], GS)
    sent(thin_got.at[others], THIN)
    for base, low_mine, mine in ((XF, low_f, part_f), (XS, low_s, part_s)):
        sent(low_mine, base)
        for c, (start, size) in enumerate(unit_cuts):
            for j in range(2):
                sent(mine.at[j, :, span(start, size)], base + 1 + 2 * c + j)
    for c, (start, size) in enumerate(unit_cuts):
        sent(part_b.at[:, span(start, size)], XB + c)
    for c, (start, size) in enumerate(width_cuts):
        more = LANES if c == nw - 1 else 0
        sent(sum_f.at[others, :, pl.ds(start, size)], RF + c)
        sent(sum_b.at[others, :, pl.ds(start, size + more)], RB + c)


def body(*args):
    fwd_input, saved, cotan, norm_gain, w_gate, w_up, w_down, adapt_a, adapt_b = args
    segments = lax.axis_size("segment")
    shards = lax.axis_size("hid")
    part, width = fwd_input.shape
    units = w_gate.shape[2]
    rank = adapt_a.shape[2]
    rows = part * shards
    wide = up_to(units, LANES)
    long = width + LANES
    nu, nw = len(cuts(units, UNIT_STEP)), len(cuts(width, WIDTH_STEP))
    groups = 9 + 4 * nu + nu + 2 * nw
    vmem = pltpu.VMEM
    gathered = vmem((shards, part, long), B16)
    pair = vmem((2, rows, wide), B16)
    single = vmem((rows, wide), B16)
    square = vmem((rows, LANES), B16)
    term = vmem((rows, units), F32)
    eight = vmem((part, width), F32)
    line = vmem((part, long), B16)
    scratch = [
        vmem((width, units), B16), vmem((width, units), B16), vmem((units, width), B16),
        vmem((width, LANES), B16), vmem((LANES, units), B16),
        gathered, gathered, gathered, vmem((rows, width), B16),
        pair, pair, pair, pair, single, single,
        square, square, square, square, square, vmem((LANES, rows), B16), vmem((rows, LANES), F32),
        vmem((rows, min(UNIT_STEP, units)), F32),
        vmem((rows, units), B16), vmem((rows, units), B16), vmem((rows, units), B16),
        term, term, term, vmem((2, rows, LANES), F32),
        gathered, gathered, gathered, gathered,
        vmem((rank, rows), F32), vmem((shards, rank, rows), F32),
        eight, eight, eight, eight,
        line, line, vmem((2, part, long), B16), eight, eight,
        pltpu.SemaphoreType.DMA((groups,)), pltpu.SemaphoreType.DMA((groups,)),
        pltpu.SemaphoreType.DMA((3,)),
    ]
    whole = pl.BlockSpec(memory_space=pltpu.VMEM)
    away = pl.BlockSpec(memory_space=pl.ANY)
    return pl.pallas_call(
        functools.partial(kernel, (segments, shards, width, units, rank)),
        out_shape=(
            jax.ShapeDtypeStruct((1, part, width), F32),
            jax.ShapeDtypeStruct((1, part, width), F32),
            jax.ShapeDtypeStruct((1, width, rank), F32),
            jax.ShapeDtypeStruct((1, rank, units), F32),
        ),
        in_specs=[whole] * 4 + [away] * 3 + [whole] * 2,
        out_specs=(whole,) * 4,
        scratch_shapes=scratch,
        compiler_params=pltpu.CompilerParams(
            collective_id=0, has_side_effects=True, vmem_limit_bytes=56 * 1024 * 1024
        ),
    )(*args)


def solution(mesh):
    placed = (
        P("hid", "wid"),
        P("segment", "hid", "wid"),
        P("hid", "wid"),
        P("segment", "wid"),
        P("segment", "wid", "hid"),
        P("segment", "wid", "hid"),
        P("segment", "hid", "wid"),
        P("segment", "wid", None),
        P("segment", None, "hid"),
    )
    return jax.shard_map(
        body,
        mesh=mesh,
        in_specs=placed,
        out_specs=(
            P("segment", "hid", "wid"),
            P("segment", "hid", "wid"),
            P("segment", "wid", None),
            P("segment", None, "hid"),
        ),
        check_vma=False,
    )
```

time: 981 us -> 186 us (0.19)
  waiting for transfers between devices: 666 us -> 0 us
  blocking collectives: 179 us -> 0 us
  Pallas kernels: 0 us -> 154 us
  matrix products: 49 us -> 0 us
  other arithmetic: 15.3 us -> 0 us
  between operations: 15.9 us -> 0.64 us
    unnamed x12 -> x0, waiting for transfers between devices: 375 us -> none
    psum x4 -> x0, waiting for transfers between devices: 279 us -> none  [body(): merged = lax.psum((terms[0], terms[1], terms[2], terms[3]), 'wid')]
    pallas_call x0 -> x1, Pallas kernels: none -> 154 us  [body(): pl.pallas_call(functools.partial(kernel, (segments, shards, width, units,...]
    all_gather x5 -> x0, blocking collectives: 121 us -> none  [the longest x4 97.4 us: body(): lax.all_gather(jnp.where(forward_on, normed, grad_round), 'hid', axis=0,...]
    psum x9 -> x0, blocking collectives: 58.3 us -> none  [the longest x4 26.1 us: body(): merged = lax.psum((terms[0], terms[1], terms[2], terms[3]), 'wid')]
    dot_general x18 -> x0, matrix products: 49 us -> none  [the longest x4 12.1 us: combine_units(): jnp.dot(round_back, adapter_b, preferred_element_type=jnp.float32)]
    ppermute x6 -> x0, waiting for transfers between devices: 11.8 us -> none  [from_behind(): return lax.ppermute(block, axis, route)]
    unnamed x80 -> x6, local copies, waits for them, and re-layouts: 32.6 us -> 28.1 us
  transfers between devices with their start and end apart: 14 -> 0, of which waited for: 14 -> 0; matrix products, arithmetic and copies ran while one was open for 0% -> 0% of each run, Pallas kernels for 0% -> 0%
where the time goes in v1:
time: 186 us; the launch traced here: 185 us
  Pallas kernels  154 us (83%)
  local copies, waits for them, and re-layouts  30.5 us (16%)
    pallas_call x1, Pallas kernels, body(): pl.pallas_call(functools.partial(kernel, (segments, shards, width, units,...  154 us
    unnamed x6, local copies, waits for them, and re-layouts  28.1 us

profile of v1, /device:TPU:0, one launch (start us, length us, event | category | flops | bytes accessed | tf_op | source)
XLA Modules:
  0.0 184.9 jit_solution(6232705046246580231)
XLA Ops:
  0.6 2.0 %copy.15.refs_7_ = bf16[1,2688,16]{2,1,0:T(8,128)(2,1)} copy(bf16[1,2688,16]{1,2,0:T(8,128)(2,1)} %param.16) | data formatting | bytes 172032 | tf_op args[7]
  2.7 10.8 %copy.13.refs_4_ = bf16[1,2688,1344]{2,1,0:T(8,128)(2,1)} copy(bf16[1,2688,1344]{1,2,0:T(8,128)(2,1)} %param.13) | data formatting | bytes 14450688 | tf_op args[4]
  13.4 10.7 %copy.14.refs_5_ = bf16[1,2688,1344]{2,1,0:T(8,128)(2,1)} copy(bf16[1,2688,1344]{1,2,0:T(8,128)(2,1)} %param.14) | data formatting | bytes 14450688 | tf_op args[5]
  24.1 153.8 %shard_map.120 = (f32[1,8,2688]{2,1,0:T(8,128)}, f32[1,8,2688]{2,1,0:T(8,128)}, f32[1,2688,16]{2,1,0:T(8,128)}, f32[1,16,1344]{2,1,0:T(8,128)}) custom-call(f32[8,2688]{1,0:T(8,128)} %refs_0_.1, f32[1,8,2688]{2,1,0:T(8,128)} %refs_1_.1, f32[8,2688]{1,0:T(8,128)} %refs_2_.1, f32[1,2688]{1,0:T(1,128)} %refs_3_.1, bf16[1,2688,1344]{2,1,0:T(8,128)(2,1)} %copy.13.refs_4_, ...), custom_call_target="tpu_custom_call" | custom-call | tf_op jit(solution)/shard_map/pallas_call | solution.py:536
  177.9 2.4 %copy.16 = f32[1,2688,16]{1,2,0:T(8,128)} copy(f32[1,2688,16]{2,1,0:T(8,128)} %get-tuple-element.6) | data formatting | bytes 344064 | tf_op jit(solution)/shard_map/pallas_call | solution.py:536
  180.3 1.5 copy.20
  181.8 1.5 copy.21
  183.4 1.5 copy.22

commit v2 on v1

v2 whole, which is shorter than its diff:
```python
import functools
import math

import jax
import jax.numpy as jnp
from jax import lax
from jax.experimental import pallas as pl
from jax.experimental.pallas import tpu as pltpu
from jax.sharding import PartitionSpec as P

EPSILON = 1e-06
LANES = 128
UNIT_STEP = 512
WIDTH_STEP = 768
ROOT = math.sqrt(2.0 / math.pi)
CUBE = 0.044715
MESH = pl.DeviceIdType.MESH
ACROSS = (((1,), (1,)), ((), ()))
F32 = jnp.float32
B16 = jnp.bfloat16


def cuts(total, step):
    return [(at, min(step, total - at)) for at in range(0, total, step)]


def up_to(size, step):
    return (size + step - 1) // step * step


def dot(a, b):
    return jnp.dot(a, b, preferred_element_type=F32)


def dot_across(a, b):
    return lax.dot_general(a, b, ACROSS, preferred_element_type=F32)


def two_parts(value):
    high = value.astype(B16).astype(F32)
    return high, value - high


def tail_of(value):
    high, low = two_parts(value)
    lane = lax.broadcasted_iota(jnp.int32, (value.shape[0], LANES), 1)
    return jnp.where(lane == 16, high, jnp.where(lane == 17, low, 0.0))


def turn_rows(value):
    return jnp.concatenate([value[..., 4:, :], value[..., :4, :]], axis=-2)


def swap(first, second):
    row = lax.broadcasted_iota(jnp.int32, first.shape, first.ndim - 2)
    upper = jnp.where(row < 4, first, turn_rows(second))
    lower = jnp.where(row < 4, turn_rows(first), second)
    return upper, lower


def kernel(sizes, *refs):
    segments, shards, width, units, rank = sizes
    (fwd_input, saved, cotan, gain, gate_hbm, up_hbm, down_hbm, adapt_a, adapt_b) = refs[:9]
    (fwd_out, grad_in, grad_a, grad_b) = refs[9:13]
    (
        w_gate, w_up, w_down, a_pad, b_pad,
        rows_f, rows_s, rows_b, flat,
        part_f, got_f, part_s, got_s, part_b, got_b,
        low_f, low_got_f, low_s, low_got_s, low_round, low_turned, inverse,
        tails, extra, hidden, d_gate, d_up, slope_term, active_term, inner_term, inner,
        sum_f, back_f, sum_b, back_b,
        thin, thin_got, x_in, g_in, x_saved, gain_here, gain_next,
        first_message, saved_message, next_message, y_out, g_out,
        sends, recvs, loads, turn,
    ) = refs[13:]
    section = lax.axis_index("segment")
    me = lax.axis_index("hid")
    side = lax.axis_index("wid")
    part = 8
    rows = part * shards
    full = width * 2
    unit_cuts = cuts(units, UNIT_STEP)
    fold = (width + LANES) // 2
    rest = width - fold
    width_cuts = cuts(fold, WIDTH_STEP)
    nu, nw = len(unit_cuts), len(width_cuts)
    batch_rows = rows // 2
    GF, GS, GB, THIN, XIN, GIN, GAIN = 0, 2, 4, 6, 7, 9, 11
    XF = 12
    XS = XF + 2 * (1 + 2 * nu)
    XB = XS + 2 * (1 + 2 * nu)
    RF = XB + 2 * nu
    RB = RF + 2 * nw

    def take(ref, sem):
        pltpu.make_async_copy(ref, ref, sem).wait()

    def weights(index):
        source, target = ((gate_hbm, w_gate), (up_hbm, w_up), (down_hbm, w_down))[index]
        return pltpu.make_async_copy(source.at[0], target, loads.at[index])

    for index in range(3):
        weights(index).start()

    barrier = pltpu.get_barrier_semaphore()

    def greet(who):
        pl.semaphore_signal(barrier, inc=1, device_id=who, device_id_type=MESH)

    def greet_peer(i, carry):
        greet({"hid": lax.rem(me + i, shards)})
        return carry

    lax.fori_loop(1, shards, greet_peer, 0)
    greet({"wid": 1 - side})

    @pl.when(section > 0)
    def _():
        def one(i, carry):
            greet({"segment": section - 1, "hid": lax.rem(me + i, shards)})
            return carry

        lax.fori_loop(0, shards, one, 0)

    @pl.when(section < segments - 1)
    def _():
        def one(i, carry):
            greet({"segment": section + 1, "hid": lax.rem(me + i, shards)})
            return carry

        lax.fori_loop(0, shards, one, 0)

    row8 = lax.broadcasted_iota(jnp.int32, (8, LANES), 0)

    def folded(values, tail):
        return swap(values[:, :fold], jnp.concatenate([values[:, fold:], tail], 1))

    def rounded(ref, values, tail):
        for batch, value in enumerate(folded(values, tail)):
            ref[batch] = value.astype(B16)

    nothing = jnp.zeros((part, LANES), F32)
    scales = jnp.broadcast_to(gain[...], (part, width))
    gain_here[...] = folded(scales, nothing)[0]
    saved_rows = saved[0]
    for batch, value in enumerate(folded(saved_rows, nothing)):
        x_saved[batch] = value

    def message(ref, x):
        rounded(ref, x * scales, tail_of(jnp.sum(x * x, axis=1, keepdims=True)))

    @pl.when(section == 0)
    def _():
        x = fwd_input[...]
        for batch, value in enumerate(folded(x, nothing)):
            x_in[batch] = value
        message(first_message, x)

    @pl.when(section == segments - 1)
    def _():
        g = cotan[...]
        for batch, value in enumerate(folded(g, nothing)):
            g_in[batch] = value
        rounded(first_message, g, nothing)

    message(saved_message, saved_rows)

    neighbours = jnp.where(section > 0, shards, 0) + jnp.where(section < segments - 1, shards, 0)
    pl.semaphore_wait(barrier, shards + neighbours)

    def spread(source, target, index, batch):
        pltpu.make_async_copy(
            source.at[batch], target.at[batch, me], recvs.at[index + batch]
        ).start()

        def one(i, carry):
            pltpu.make_async_remote_copy(
                src_ref=source.at[batch], dst_ref=target.at[batch, me],
                send_sem=sends.at[index + batch], recv_sem=recvs.at[index + batch],
                device_id={"hid": lax.rem(me + i, shards)}, device_id_type=MESH,
            ).start()
            return carry

        lax.fori_loop(1, shards, one, 0)

    def spread_both(source, target, index):
        for batch in range(2):
            spread(source, target, index, batch)

    def spread_to(other, source, target, index, batch):
        def one(i, carry):
            pltpu.make_async_remote_copy(
                src_ref=source.at[batch], dst_ref=target.at[batch, me],
                send_sem=sends.at[index + batch], recv_sem=recvs.at[index + batch],
                device_id={"segment": other, "hid": lax.rem(me + i, shards)}, device_id_type=MESH,
            ).start()
            return carry

        lax.fori_loop(0, shards, one, 0)

    def deliver(source, target, index, batch, columns):
        pltpu.make_async_copy(
            source.at[batch, me, :, columns], target.at[batch, me, :, columns], recvs.at[index]
        ).start()

        def one(i, carry):
            peer = lax.rem(me + i, shards)
            pltpu.make_async_remote_copy(
                src_ref=source.at[batch, peer, :, columns],
                dst_ref=target.at[batch, me, :, columns],
                send_sem=sends.at[index], recv_sem=recvs.at[index],
                device_id={"hid": peer}, device_id_type=MESH,
            ).start()
            return carry

        lax.fori_loop(1, shards, one, 0)

    def across(source, target, index):
        return pltpu.make_async_remote_copy(
            src_ref=source, dst_ref=target,
            send_sem=sends.at[index], recv_sem=recvs.at[index],
            device_id={"wid": 1 - side}, device_id_type=MESH,
        )

    def onward(other, source, target, index):
        return pltpu.make_async_remote_copy(
            src_ref=source, dst_ref=target,
            send_sem=sends.at[index], recv_sem=recvs.at[index],
            device_id={"segment": other}, device_id_type=MESH,
        )

    @pl.when(section == 0)
    def _():
        spread(first_message, rows_f, GF, 0)

    @pl.when(section == segments - 1)
    def _():
        spread_both(saved_message, rows_s, GS)
        spread_both(first_message, rows_b, GB)

    @pl.when(section > 0)
    def _():
        onward(section - 1, gain_here, gain_next, GAIN).start()

    a_pad[...] = jnp.zeros_like(a_pad)
    a_pad[:rank, :] = adapt_a[0]
    b_pad[...] = jnp.zeros_like(b_pad)
    b_pad[:rank, :] = adapt_b[0]
    wide = part_f.shape[2]
    last = units // LANES * LANES
    if last < wide:
        for buffer in (part_f, part_s):
            for j in range(2):
                buffer[j, :, last:] = jnp.zeros((rows, wide - last), B16)
        part_b[:, last:] = jnp.zeros((rows, wide - last), B16)

    def rows_of(batch):
        return slice(batch * batch_rows, (batch + 1) * batch_rows)

    @pl.when(section == 0)
    def _():
        spread(first_message, rows_f, GF, 1)

    def flatten(source, batch):
        def one(i, carry):
            lefts, rights = [], []
            for j in range(2):
                pair = [source[batch, 4 * i + 2 * j + k].astype(F32) for k in range(2)]
                left, right = swap(pair[0], pair[1])
                lefts.append(left)
                rights.append(right)
            at_rows = pl.ds(pl.multiple_of(batch * batch_rows + i * 16, 16), 16)
            right = jnp.concatenate(rights, 0)
            flat[at_rows, :fold] = jnp.concatenate(lefts, 0).astype(B16)
            flat[at_rows, fold:] = right[:, :rest].astype(B16)
            tails[at_rows, :] = right[:, rest:]
            return carry

        lax.fori_loop(0, shards // 4, one, 0)

    def span(start, size):
        return pl.ds(start, up_to(size, LANES))

    def arrived(gathered, index, batch):
        take(gathered.at[batch], recvs.at[index + batch])
        flatten(gathered, batch)

    def project(gathered, index, mine, theirs, low_mine, low_theirs, base, batches):
        step = 1 + 2 * nu
        here = slice(batches[0] * batch_rows, (batches[-1] + 1) * batch_rows)
        for batch in batches:
            arrived(gathered, index, batch)
        low_mine[here, :] = (dot_across(flat[here, :], a_pad[...]) + tails[here, :]).astype(B16)
        for batch in batches:
            ours = rows_of(batch)
            across(low_mine.at[ours], low_theirs.at[ours], base + batch * step).start()
        for c, (start, size) in enumerate(unit_cuts):
            for j, matrix in enumerate((w_gate, w_up)):
                mine[j, here, start : start + size] = dot_across(
                    flat[here, :], matrix[start : start + size, :]
                ).astype(B16)
                for batch in batches:
                    ours = rows_of(batch)
                    across(
                        mine.at[j, ours, span(start, size)],
                        theirs.at[j, ours, span(start, size)],
                        base + batch * step + 1 + 2 * c + j,
                    ).start()

    def join_low(low_mine, low_theirs, base, batch):
        base = base + batch * (1 + 2 * nu)
        here = rows_of(batch)
        take(low_theirs.at[here], recvs.at[base])
        low = low_mine[here, :].astype(F32) + low_theirs[here, :].astype(F32)
        squares = low[:, 16:17] + low[:, 17:18]
        inv = lax.rsqrt(squares / full + EPSILON)
        inverse[here, :] = jnp.broadcast_to(inv, (batch_rows, LANES))
        lane = lax.broadcasted_iota(jnp.int32, (batch_rows, LANES), 1)
        low_round[here, :] = jnp.where(lane < rank, low * inv, 0.0).astype(B16)

    def each_block(work, batch):
        def one(i, carry):
            work(pl.ds(pl.multiple_of(batch * batch_rows + i * 16, 16), 16), i)
            return carry

        lax.fori_loop(0, batch_rows // 16, one, 0)

    def join_units(mine, theirs, base, work, batch):
        base = base + batch * (1 + 2 * nu)
        rows_here = rows_of(batch)
        for c, (start, size) in enumerate(unit_cuts):
            for j in range(2):
                take(theirs.at[j, rows_here, span(start, size)], recvs.at[base + 1 + 2 * c + j])
            extra[:, :size] = dot(low_round[rows_here, :], b_pad[:, start : start + size])
            here = slice(start, start + size)

            def block(at_rows, i):
                inv = inverse[at_rows, :1]
                gate = mine[0, at_rows, here].astype(F32) + theirs[0, at_rows, here].astype(F32)
                up = mine[1, at_rows, here].astype(F32) + theirs[1, at_rows, here].astype(F32)
                added = extra[pl.ds(pl.multiple_of(i * 16, 16), 16), :size]
                work(at_rows, here, gate * inv, up * inv + added)

            each_block(block, batch)

    def pack(target, batch, start, size, left, right):
        shape = (shards // 2, 8, size)
        even, odd = swap(left.reshape(shape), right.reshape(shape))
        for i in range(shards // 2):
            target[batch, 2 * i, :, start : start + size] = even[i].astype(B16)
            target[batch, 2 * i + 1, :, start : start + size] = odd[i].astype(B16)

    def total(received, index, batch):
        parts = []
        for c, (start, size) in enumerate(width_cuts):
            take(received.at[batch, :, :, pl.ds(start, size)], recvs.at[index + batch * nw + c])
            value = received[batch, 0, :, start : start + size].astype(F32)
            for k in range(1, shards):
                value = value + received[batch, k, :, start : start + size].astype(F32)
            parts.append(value)
        return jnp.concatenate(parts, 1)

    def send_on(other, values, tail, batch, slot, target, index):
        message_ref = next_message.at[slot]
        message_ref[batch, :, :rest] = values[:, :rest].astype(B16)
        message_ref[batch, :, rest:] = jnp.where(row8 < 4, values[:, rest:], tail).astype(B16)
        spread_to(other, message_ref, target, index, batch)

    def unfold(target, blocks):
        left, right = swap(blocks[0], blocks[1])
        target[0, :, :fold] = left
        target[0, :, fold:] = right[:, :rest]

    def forward():
        for batch in range(2):
            project(rows_f, GF, part_f, got_f, low_f, low_got_f, XF, (batch,))

        @pl.when(section == 1)
        def _():
            spread_both(saved_message, rows_s, GS)

        def work(at_rows, here, gate, up):
            bend = jnp.tanh(ROOT * (gate + CUBE * gate * gate * gate))
            hidden[at_rows, here] = (0.5 * gate * (1.0 + bend) * up).astype(B16)

        for batch in range(2):
            join_low(low_f, low_got_f, XF, batch)
            join_units(part_f, got_f, XF, work, batch)
            h = hidden[rows_of(batch), :]
            for c, (start, size) in enumerate(width_cuts):
                left = dot(h, w_down[:, start : start + size])
                real = min(size, rest - start)
                right = dot(h, w_down[:, fold + start : fold + start + real])
                if real < size:
                    right = jnp.concatenate([right, jnp.zeros((batch_rows, size - real), F32)], 1)
                pack(sum_f, batch, start, size, left, right)
                deliver(sum_f, back_f, RF + batch * nw + c, batch, pl.ds(start, size))

        @pl.when(section < segments - 1)
        def _():
            take(gain_next, recvs.at[GAIN])

        for batch in range(2):

            @pl.when(section > 0)
            def _():
                take(x_in.at[batch], recvs.at[XIN + batch])

            value = total(back_f, RF, batch)
            bottom = jnp.where(row8 < 4, value[:, rest:], 0.0)
            y = x_in[batch] + jnp.concatenate([value[:, :rest], bottom], 1)
            y_out[batch] = y

            @pl.when(section < segments - 1)
            def _():
                squares = jnp.sum(y * y, axis=1, keepdims=True)
                tail = tail_of(squares + turn_rows(squares))
                send_on(section + 1, y * gain_next[...], tail, batch, 0, rows_f, GF)
                onward(section + 1, y_out.at[batch], x_in.at[batch], XIN + batch).start()

        unfold(fwd_out, (y_out[0], y_out[1]))

    def recompute():
        @pl.when(jnp.logical_or(section == 0, section == 2))
        def _():
            pl.semaphore_wait(turn, 1)
            spread_both(saved_message, rows_s, GS)

        project(rows_s, GS, part_s, got_s, low_s, low_got_s, XS, (0, 1))

        @pl.when(section == 1)
        def _():
            pl.semaphore_signal(turn, inc=1, device_id={"segment": 0}, device_id_type=MESH)

    def join_saved():
        def work(at_rows, here, gate, up):
            bend = jnp.tanh(ROOT * (gate + CUBE * gate * gate * gate))
            active = 0.5 * gate * (1.0 + bend)
            slope = 0.5 * (1.0 + bend) + 0.5 * gate * (1.0 - bend * bend) * (
                ROOT * (1.0 + 3.0 * CUBE * gate * gate)
            )
            steep = up * slope
            slope_term[at_rows, here] = steep
            active_term[at_rows, here] = active
            inner_term[at_rows, here] = steep * gate + active * up

        for batch in range(2):
            join_low(low_s, low_got_s, XS, batch)
            join_units(part_s, got_s, XS, work, batch)
        inner[1] = inverse[...]
        low_turned[...] = low_round[...].astype(F32).T.astype(B16)

    def backward():
        for batch in range(2):
            arrived(rows_b, GB, batch)
            at_rows = rows_of(batch)
            for c, (start, size) in enumerate(unit_cuts):
                part_b[at_rows, start : start + size] = dot_across(
                    flat[at_rows, :], w_down[start : start + size, :]
                ).astype(B16)
                across(
                    part_b.at[at_rows, span(start, size)],
                    got_b.at[at_rows, span(start, size)],
                    XB + batch * nu + c,
                ).start()

        @pl.when(section == segments - 1)
        def _():
            pl.semaphore_signal(turn, inc=1, device_id={"segment": 2}, device_id_type=MESH)

        join_saved()
        inner[0] = jnp.zeros((rows, LANES), F32)
        for batch in range(2):
            ours = rows_of(batch)
            for c, (start, size) in enumerate(unit_cuts):
                take(got_b.at[ours, span(start, size)], recvs.at[XB + batch * nu + c])
                here = slice(start, start + size)

                def block(at_rows, i):
                    d_hid = part_b[at_rows, here].astype(F32) + got_b[at_rows, here].astype(F32)
                    d_gate[at_rows, here] = (d_hid * slope_term[at_rows, here]).astype(B16)
                    d_up[at_rows, here] = (d_hid * active_term[at_rows, here]).astype(B16)
                    inner[0, at_rows, :] += jnp.broadcast_to(
                        jnp.sum(d_hid * inner_term[at_rows, here], axis=1, keepdims=True),
                        (16, LANES),
                    )

                each_block(block, batch)
            d_low_round = dot_across(d_up[ours, :], b_pad[...]).astype(B16)
            tail = tail_of(inner[0, ours, :1])

            def product(start, size):
                here = slice(start, start + size)
                value = dot(d_gate[ours, :], w_gate[:, here])
                value = value + dot(d_up[ours, :], w_up[:, here])
                return value + dot(d_low_round, a_pad[:, here])

            for c, (start, size) in enumerate(width_cuts):
                left = product(start, size)
                real = min(size, rest - start)
                right = product(fold + start, real)
                if real < size:
                    right = jnp.concatenate([right, tail], 1)
                pack(sum_b, batch, start, size, left, right)
                deliver(sum_b, back_b, RB + batch * nw + c, batch, pl.ds(start, size))
        d_low = dot_across(d_up[...], b_pad[...])
        thin[...] = (d_low * inner[1]).T[:rank]

        def one(i, carry):
            pltpu.make_async_remote_copy(
                src_ref=thin, dst_ref=thin_got.at[me],
                send_sem=sends.at[THIN], recv_sem=recvs.at[THIN],
                device_id={"hid": lax.rem(me + i, shards)}, device_id_type=MESH,
            ).start()
            return carry

        pltpu.make_async_copy(thin, thin_got.at[me], recvs.at[THIN]).start()
        lax.fori_loop(1, shards, one, 0)
        grad_b[0] = dot(low_turned[...], d_up[...])[:rank]

        for batch in range(2):

            @pl.when(section < segments - 1)
            def _():
                take(g_in.at[batch], recvs.at[GIN + batch])

            at_row = pl.multiple_of(batch * batch_rows + me // 2 * 8, 8)
            inv = inner[1, pl.ds(at_row, 8), :]
            upper = jnp.where(lax.rem(me, 2) == 0, 0, 4)
            inv = jnp.where(row8 // 4 * 4 == upper, inv, turn_rows(inv))[:, :1]
            value = total(back_b, RB, batch)
            weight = value[:, rest + 16 : rest + 17] + value[:, rest + 17 : rest + 18]
            weight = jnp.where(row8 < 4, turn_rows(weight), weight)[:, :1]
            weight = inv * inv * weight / full
            g = g_in[batch] + inv * gain_here[...] * value - x_saved[batch] * weight
            g_out[batch] = g

            @pl.when(section > 0)
            def _():
                send_on(section - 1, g, nothing, batch, 1, rows_b, GB)
                onward(section - 1, g_out.at[batch], g_in.at[batch], GIN + batch).start()

        unfold(grad_in, (g_out[0], g_out[1]))
        take(thin_got, recvs.at[THIN])
        low_sum = thin_got[0]
        for k in range(1, shards):
            low_sum = low_sum + thin_got[k]
        high, low = two_parts(low_sum)
        for batch in range(2):
            flatten(rows_s, batch)
        grad_a[0] = dot(high.astype(B16), flat[...]) + dot(low.astype(B16), flat[...])

    for index in range(3):
        weights(index).wait()

    def moment(now, carry):
        pl.when(section == now)(forward)
        pl.when(now == jnp.where(section == 1, 1, 0))(recompute)
        pl.when(section == segments - 1 - now)(backward)
        return carry

    lax.fori_loop(0, segments, moment, 0)

    def sent(ref, index):
        take(ref, sends.at[index])

    others = pl.ds(0, shards - 1)
    for batch in range(2):

        @pl.when(section < segments - 1)
        def _():
            sent(rows_f.at[batch], GF + batch)
            sent(y_out.at[batch], XIN + batch)

        @pl.when(section > 0)
        def _():
            sent(rows_b.at[batch], GB + batch)
            sent(g_out.at[batch], GIN + batch)

        @pl.when(section == 0)
        def _():
            sent(rows_f.at[batch, others], GF + batch)

        @pl.when(section == segments - 1)
        def _():
            sent(rows_b.at[batch, others], GB + batch)

        sent(rows_s.at[batch, others], GS + batch)

    @pl.when(section > 0)
    def _():
        sent(gain_here, GAIN)

    sent(thin_got.at[others], THIN)
    for batch in range(2):
        here = rows_of(batch)
        for first, low_mine, mine in ((XF, low_f, part_f), (XS, low_s, part_s)):
            base = first + batch * (1 + 2 * nu)
            sent(low_mine.at[here], base)
            for c, (start, size) in enumerate(unit_cuts):
                for j in range(2):
                    sent(mine.at[j, here, span(start, size)], base + 1 + 2 * c + j)
        for c, (start, size) in enumerate(unit_cuts):
            sent(part_b.at[here, span(start, size)], XB + batch * nu + c)
    for batch in range(2):
        for c, (start, size) in enumerate(width_cuts):
            columns = pl.ds(start, size)
            sent(sum_f.at[batch, others, :, columns], RF + batch * nw + c)
            sent(sum_b.at[batch, others, :, columns], RB + batch * nw + c)


def hand_over(*refs):
    for source, target in zip(refs[:4], refs[4:]):
        target[...] = source[...]


def body(*args):
    fwd_input, saved, cotan, norm_gain, w_gate, w_up, w_down, adapt_a, adapt_b = args
    segments = lax.axis_size("segment")
    shards = lax.axis_size("hid")
    part, width = fwd_input.shape
    units = w_gate.shape[2]
    rank = adapt_a.shape[2]
    rows = part * shards
    wide = up_to(units, LANES)
    fold = (width + LANES) // 2
    nu, nw = len(cuts(units, UNIT_STEP)), len(cuts(fold, WIDTH_STEP))
    groups = 12 + 4 * (1 + 2 * nu) + 2 * nu + 4 * nw
    vmem = pltpu.VMEM
    gathered = vmem((2, shards, part, fold), B16)
    pair = vmem((2, rows, wide), B16)
    single = vmem((rows, wide), B16)
    square = vmem((rows, LANES), B16)
    term = vmem((rows, units), F32)
    block = vmem((part, fold), F32)
    pair_block = vmem((2, part, fold), F32)
    line = vmem((2, part, fold), B16)
    scratch = [
        vmem((units, width), B16), vmem((units, width), B16), vmem((units, width), B16),
        vmem((LANES, width), B16), vmem((LANES, units), B16),
        gathered, gathered, gathered, vmem((rows, width), B16),
        pair, pair, pair, pair, single, single,
        square, square, square, square, square, vmem((LANES, rows), B16), vmem((rows, LANES), F32),
        vmem((rows, LANES), F32), vmem((rows // 2, min(UNIT_STEP, units)), F32),
        vmem((rows, units), B16), vmem((rows, units), B16), vmem((rows, units), B16),
        term, term, term, vmem((2, rows, LANES), F32),
        gathered, gathered, gathered, gathered,
        vmem((rank, rows), F32), vmem((shards, rank, rows), F32),
        pair_block, pair_block, pair_block, block, block,
        line, line, vmem((2, 2, part, fold), B16), pair_block, pair_block,
        pltpu.SemaphoreType.DMA((groups,)), pltpu.SemaphoreType.DMA((groups,)),
        pltpu.SemaphoreType.DMA((3,)), pltpu.SemaphoreType.REGULAR,
    ]
    whole = pl.BlockSpec(memory_space=pltpu.VMEM)
    away = pl.BlockSpec(memory_space=pl.ANY)
    results = pl.pallas_call(
        functools.partial(kernel, (segments, shards, width, units, rank)),
        out_shape=(
            jax.ShapeDtypeStruct((1, part, width), F32),
            jax.ShapeDtypeStruct((1, part, width), F32),
            jax.ShapeDtypeStruct((1, rank, width), F32),
            jax.ShapeDtypeStruct((1, rank, units), F32),
        ),
        in_specs=[whole] * 4 + [away] * 3 + [whole] * 2,
        out_specs=(whole,) * 4,
        scratch_shapes=scratch,
        compiler_params=pltpu.CompilerParams(
            collective_id=0, has_side_effects=True, vmem_limit_bytes=56 * 1024 * 1024
        ),
    )(
        fwd_input, saved, cotan, norm_gain, jnp.swapaxes(w_gate, 1, 2), jnp.swapaxes(w_up, 1, 2),
        w_down, jnp.swapaxes(adapt_a, 1, 2), adapt_b,
    )
    fwd_out, grad_in, grad_a, grad_b = pl.pallas_call(
        hand_over,
        out_shape=tuple(jax.ShapeDtypeStruct(value.shape, value.dtype) for value in results),
        in_specs=[whole] * 4,
        out_specs=(whole,) * 4,
    )(*results)
    return fwd_out, grad_in, jnp.swapaxes(grad_a, 1, 2), grad_b


def solution(mesh):
    placed = (
        P("hid", "wid"),
        P("segment", "hid", "wid"),
        P("hid", "wid"),
        P("segment", "wid"),
        P("segment", "wid", "hid"),
        P("segment", "wid", "hid"),
        P("segment", "hid", "wid"),
        P("segment", "wid", None),
        P("segment", None, "hid"),
    )
    return jax.shard_map(
        body,
        mesh=mesh,
        in_specs=placed,
        out_specs=(
            P("segment", "hid", "wid"),
            P("segment", "hid", "wid"),
            P("segment", "wid", None),
            P("segment", None, "hid"),
        ),
        check_vma=False,
    )
```

time: 186 us -> 134 us (0.72)
  local copies, waits for them, and re-layouts: 30.5 us -> 0 us
  Pallas kernels: 154 us -> 133 us
    unnamed x6 -> x0, local copies, waits for them, and re-layouts: 28.1 us -> none
    pallas_call x1, Pallas kernels: 154 us -> 131 us  [body(): pl.pallas_call(functools.partial(kernel, (segments, shards, width, units,...]
    pallas_call x1 -> x0, local copies, waits for them, and re-layouts: 2.42 us -> none  [body(): pl.pallas_call(functools.partial(kernel, (segments, shards, width, units,...]
where the time goes in v2:
time: 134 us; the launch traced here: 133 us
  Pallas kernels  133 us (99%)
    pallas_call x1, Pallas kernels, body(): pl.pallas_call(functools.partial(kernel, (segments, shards, width, units,...  131 us

profile of v2, /device:TPU:0, one launch (start us, length us, event | category | flops | bytes accessed | tf_op | source)
XLA Modules:
  0.0 133.4 jit_solution(16213042972578063909)
XLA Ops:
  0.6 130.9 %shard_map.120 = (f32[1,8,2688]{2,1,0:T(8,128)}, f32[1,8,2688]{2,1,0:T(8,128)}, f32[1,16,2688]{2,1,0:T(8,128)}, f32[1,16,1344]{2,1,0:T(8,128)}) custom-call(f32[8,2688]{1,0:T(8,128)} %refs_0_.1, f32[1,8,2688]{2,1,0:T(8,128)} %refs_1_.1, f32[8,2688]{1,0:T(8,128)} %refs_2_.1, f32[1,2688]{1,0:T(1,128)} %refs_3_.1, bf16[1,1344,2688]{2,1,0:T(8,128)(2,1)} %bitcast.4, ...), custom_call_target="tpu_custom_call" | custom-call | tf_op jit(solution)/shard_map/pallas_call | solution.py:656
  131.6 1.8 %shard_map.121 = (f32[1,8,2688]{2,1,0:T(8,128)}, f32[1,8,2688]{2,1,0:T(8,128)}, f32[1,16,2688]{2,1,0:T(8,128)}, f32[1,16,1344]{2,1,0:T(8,128)}) custom-call(f32[1,8,2688]{2,1,0:T(8,128)} %get-tuple-element.12.refs_0_, f32[1,8,2688]{2,1,0:T(8,128)} %get-tuple-element.13.refs_1_, f32[1,16,2688]{2,1,0:T(8,128)} %get-tuple-element.14.refs_2_, ...), custom_call_target="tpu_custom_call" | custom-call | tf_op jit(solution)/shard_map/pallas_call | solution.py:674

commit v3 on v2

--- a/solution.py
+++ b/solution.py
@@ -10,7 +10,7 @@
 
 EPSILON = 1e-06
 LANES = 128
-UNIT_STEP = 512
+UNIT_STEP = 1344
 WIDTH_STEP = 768
 ROOT = math.sqrt(2.0 / math.pi)
 CUBE = 0.044715
@@ -66,7 +66,7 @@
         w_gate, w_up, w_down, a_pad, b_pad,
         rows_f, rows_s, rows_b, flat,
         part_f, got_f, part_s, got_s, part_b, got_b,
-        low_f, low_got_f, low_s, low_got_s, low_round, low_turned, inverse,
+        low_f, low_got_f, low_s, low_got_s, low_round, low_turned, inverse, d_low,
         tails, extra, hidden, d_gate, d_up, slope_term, active_term, inner_term, inner,
         sum_f, back_f, sum_b, back_b,
         thin, thin_got, x_in, g_in, x_saved, gain_here, gain_next,
@@ -236,7 +236,6 @@
     @pl.when(section == segments - 1)
     def _():
         spread_both(saved_message, rows_s, GS)
-        spread_both(first_message, rows_b, GB)
 
     @pl.when(section > 0)
     def _():
@@ -260,6 +259,10 @@
     @pl.when(section == 0)
     def _():
         spread(first_message, rows_f, GF, 1)
+
+    @pl.when(section == segments - 1)
+    def _():
+        spread_both(first_message, rows_b, GB)
 
     def flatten(source, batch):
         def one(i, carry):
@@ -450,9 +453,34 @@
         inner[1] = inverse[...]
         low_turned[...] = low_round[...].astype(F32).T.astype(B16)
 
+    def thin_to(i, carry):
+        pltpu.make_async_remote_copy(
+            src_ref=thin, dst_ref=thin_got.at[me],
+            send_sem=sends.at[THIN], recv_sem=recvs.at[THIN],
+            device_id={"hid": lax.rem(me + i, shards)}, device_id_type=MESH,
+        ).start()
+        return carry
+
+    def adapter_gradient():
+        take(thin_got, recvs.at[THIN])
+        low_sum = thin_got[0]
+        for k in range(1, shards):
+            low_sum = low_sum + thin_got[k]
+        high, low = two_parts(low_sum)
+        for batch in range(2):
+            flatten(rows_s, batch)
+        grad_a[0] = dot(high.astype(B16), flat[...]) + dot(low.astype(B16), flat[...])
+
+    def hand_turn():
+        @pl.when(section == segments - 1)
+        def _():
+            pl.semaphore_signal(turn, inc=1, device_id={"segment": 2}, device_id_type=MESH)
+
     def backward():
         for batch in range(2):
             arrived(rows_b, GB, batch)
+            if batch == 1:
+                hand_turn()
             at_rows = rows_of(batch)
             for c, (start, size) in enumerate(unit_cuts):
                 part_b[at_rows, start : start + size] = dot_across(
@@ -464,10 +492,6 @@
                     XB + batch * nu + c,
                 ).start()
 
-        @pl.when(section == segments - 1)
-        def _():
-            pl.semaphore_signal(turn, inc=1, device_id={"segment": 2}, device_id_type=MESH)
-
         join_saved()
         inner[0] = jnp.zeros((rows, LANES), F32)
         for batch in range(2):
@@ -486,7 +510,12 @@
                     )
 
                 each_block(block, batch)
-            d_low_round = dot_across(d_up[ours, :], b_pad[...]).astype(B16)
+            d_low[ours, :] = dot_across(d_up[ours, :], b_pad[...])
+            d_low_round = d_low[ours, :].astype(B16)
+            if batch == 1:
+                thin[...] = (d_low[...] * inner[1]).T[:rank]
+                pltpu.make_async_copy(thin, thin_got.at[me], recvs.at[THIN]).start()
+                lax.fori_loop(1, shards, thin_to, 0)
             tail = tail_of(inner[0, ours, :1])
 
             def product(start, size):
@@ -503,19 +532,6 @@
                     right = jnp.concatenate([right, tail], 1)
                 pack(sum_b, batch, start, size, left, right)
                 deliver(sum_b, back_b, RB + batch * nw + c, batch, pl.ds(start, size))
-        d_low = dot_across(d_up[...], b_pad[...])
-        thin[...] = (d_low * inner[1]).T[:rank]
-
-        def one(i, carry):
-            pltpu.make_async_remote_copy(
-                src_ref=thin, dst_ref=thin_got.at[me],
-                send_sem=sends.at[THIN], recv_sem=recvs.at[THIN],
-                device_id={"hid": lax.rem(me + i, shards)}, device_id_type=MESH,
-            ).start()
-            return carry
-
-        pltpu.make_async_copy(thin, thin_got.at[me], recvs.at[THIN]).start()
-        lax.fori_loop(1, shards, one, 0)
         grad_b[0] = dot(low_turned[...], d_up[...])[:rank]
 
         for batch in range(2):
@@ -524,6 +540,8 @@
             def _():
                 take(g_in.at[batch], recvs.at[GIN + batch])
 
+            if batch == 1:
+                adapter_gradient()
             at_row = pl.multiple_of(batch * batch_rows + me // 2 * 8, 8)
             inv = inner[1, pl.ds(at_row, 8), :]
             upper = jnp.where(lax.rem(me, 2) == 0, 0, 4)
@@ -541,14 +559,6 @@
                 onward(section - 1, g_out.at[batch], g_in.at[batch], GIN + batch).start()
 
         unfold(grad_in, (g_out[0], g_out[1]))
-        take(thin_got, recvs.at[THIN])
-        low_sum = thin_got[0]
-        for k in range(1, shards):
-            low_sum = low_sum + thin_got[k]
-        high, low = two_parts(low_sum)
-        for batch in range(2):
-            flatten(rows_s, batch)
-        grad_a[0] = dot(high.astype(B16), flat[...]) + dot(low.astype(B16), flat[...])
 
     for index in range(3):
         weights(index).wait()
@@ -640,7 +650,7 @@
         vmem((LANES, width), B16), vmem((LANES, units), B16),
         gathered, gathered, gathered, vmem((rows, width), B16),
         pair, pair, pair, pair, single, single,
-        square, square, square, square, square, vmem((LANES, rows), B16), vmem((rows, LANES), F32),
+        square, square, square, square, square, vmem((LANES, rows), B16), vmem((rows, LANES), F32), vmem((rows, LANES), F32),
         vmem((rows, LANES), F32), vmem((rows // 2, min(UNIT_STEP, units)), F32),
         vmem((rows, units), B16), vmem((rows, units), B16), vmem((rows, units), B16),
         term, term, term, vmem((2, rows, LANES), F32),

time: 134 us -> 124 us (0.925)
  Pallas kernels: 133 us -> 122 us
    pallas_call x1, Pallas kernels: 131 us -> 120 us  [body(): pl.pallas_call(functools.partial(kernel, (segments, shards, width, units,...]
where the time goes in v3:
time: 124 us; the launch traced here: 123 us
  Pallas kernels  122 us (98%)
    pallas_call x1, Pallas kernels, body(): pl.pallas_call(functools.partial(kernel, (segments, shards, width, units,...  120 us

profile of v3, /device:TPU:0, one launch (start us, length us, event | category | flops | bytes accessed | tf_op | source)
XLA Modules:
  0.0 122.9 jit_solution(14048725478889841588)
XLA Ops:
  0.6 120.5 %shard_map.120 = (f32[1,8,2688]{2,1,0:T(8,128)}, f32[1,8,2688]{2,1,0:T(8,128)}, f32[1,16,2688]{2,1,0:T(8,128)}, f32[1,16,1344]{2,1,0:T(8,128)}) custom-call(f32[8,2688]{1,0:T(8,128)} %refs_0_.1, f32[1,8,2688]{2,1,0:T(8,128)} %refs_1_.1, f32[8,2688]{1,0:T(8,128)} %refs_2_.1, f32[1,2688]{1,0:T(1,128)} %refs_3_.1, bf16[1,1344,2688]{2,1,0:T(8,128)(2,1)} %bitcast.4, ...), custom_call_target="tpu_custom_call" | custom-call | tf_op jit(solution)/shard_map/pallas_call | solution.py:666
  121.1 1.8 %shard_map.121 = (f32[1,8,2688]{2,1,0:T(8,128)}, f32[1,8,2688]{2,1,0:T(8,128)}, f32[1,16,2688]{2,1,0:T(8,128)}, f32[1,16,1344]{2,1,0:T(8,128)}) custom-call(f32[1,8,2688]{2,1,0:T(8,128)} %get-tuple-element.12.refs_0_, f32[1,8,2688]{2,1,0:T(8,128)} %get-tuple-element.13.refs_1_, f32[1,16,2688]{2,1,0:T(8,128)} %get-tuple-element.14.refs_2_, ...), custom_call_target="tpu_custom_call" | custom-call | tf_op jit(solution)/shard_map/pallas_call | solution.py:684

commit v4 on v3

--- a/solution.py
+++ b/solution.py
@@ -99,7 +99,7 @@
         source, target = ((gate_hbm, w_gate), (up_hbm, w_up), (down_hbm, w_down))[index]
         return pltpu.make_async_copy(source.at[0], target, loads.at[index])
 
-    for index in range(3):
+    for index in range(2):
         weights(index).start()
 
     barrier = pltpu.get_barrier_semaphore()
@@ -240,6 +240,8 @@
     @pl.when(section > 0)
     def _():
         onward(section - 1, gain_here, gain_next, GAIN).start()
+
+    weights(2).start()
 
     a_pad[...] = jnp.zeros_like(a_pad)
     a_pad[:rank, :] = adapt_a[0]
@@ -378,6 +380,10 @@
         for batch in range(2):
             project(rows_f, GF, part_f, got_f, low_f, low_got_f, XF, (batch,))
 
+        @pl.when(section <= 1)
+        def _():
+            weights(2).wait()
+
         @pl.when(section == 1)
         def _():
             spread_both(saved_message, rows_s, GS)
@@ -430,6 +436,10 @@
             spread_both(saved_message, rows_s, GS)
 
         project(rows_s, GS, part_s, got_s, low_s, low_got_s, XS, (0, 1))
+
+        @pl.when(section >= 2)
+        def _():
+            weights(2).wait()
 
         @pl.when(section == 1)
         def _():
@@ -560,7 +570,7 @@
 
         unfold(grad_in, (g_out[0], g_out[1]))
 
-    for index in range(3):
+    for index in range(2):
         weights(index).wait()
 
     def moment(now, carry):

time: 124 us -> 124 us (level)
  no operation moved by 1% of the time
where the time goes in v4:
time: 124 us; the launch traced here: 123 us
  Pallas kernels  122 us (98%)
    pallas_call x1, Pallas kernels, body(): pl.pallas_call(functools.partial(kernel, (segments, shards, width, units,...  120 us

profile of v4, /device:TPU:0, one launch (start us, length us, event | category | flops | bytes accessed | tf_op | source)
XLA Modules:
  0.0 122.9 jit_solution(7172113124068773828)
XLA Ops:
  0.6 120.5 %shard_map.120 = (f32[1,8,2688]{2,1,0:T(8,128)}, f32[1,8,2688]{2,1,0:T(8,128)}, f32[1,16,2688]{2,1,0:T(8,128)}, f32[1,16,1344]{2,1,0:T(8,128)}) custom-call(f32[8,2688]{1,0:T(8,128)} %refs_0_.1, f32[1,8,2688]{2,1,0:T(8,128)} %refs_1_.1, f32[8,2688]{1,0:T(8,128)} %refs_2_.1, f32[1,2688]{1,0:T(1,128)} %refs_3_.1, bf16[1,1344,2688]{2,1,0:T(8,128)(2,1)} %bitcast.4, ...), custom_call_target="tpu_custom_call" | custom-call | tf_op jit(solution)/shard_map/pallas_call | solution.py:676
  121.1 1.8 %shard_map.121 = (f32[1,8,2688]{2,1,0:T(8,128)}, f32[1,8,2688]{2,1,0:T(8,128)}, f32[1,16,2688]{2,1,0:T(8,128)}, f32[1,16,1344]{2,1,0:T(8,128)}) custom-call(f32[1,8,2688]{2,1,0:T(8,128)} %get-tuple-element.12.refs_0_, f32[1,8,2688]{2,1,0:T(8,128)} %get-tuple-element.13.refs_1_, f32[1,16,2688]{2,1,0:T(8,128)} %get-tuple-element.14.refs_2_, ...), custom_call_target="tpu_custom_call" | custom-call | tf_op jit(solution)/shard_map/pallas_call | solution.py:694
